TPU v7x, 32 devices: a whole 2x2x4 slice. The times are simulated.
32 devices in a mesh: ctx: 8 (over y, x, core), grp: 4 (over z).
Axes of the slice: x: 2, y: 2, z: 4, core: 2. Of those that a mesh axis runs over, the one named last changes fastest.
Arguments:
- queries: bfloat16 [1024, 4096], P('ctx', 'grp'), may hold values from -96 to 96
- key_value_pair: bfloat16 [1024, 2, 512], P('ctx', None, 'grp'), may hold values from -4 to 4
- attention_upstream: bfloat16 [1024, 4096], P('ctx', 'grp'), may hold values from -6 to 6
- ssm_input: bfloat16 [1024, 4096], P('ctx', 'grp'), may hold values from -6 to 6
- write_vec: bfloat16 [1024, 256], P('ctx'), may hold values from -0.375 to 0.375
- read_vec: bfloat16 [1024, 256], P('ctx'), may hold values from -0.375 to 0.375
- log_decay: float32 [1024, 64], P('ctx', 'grp'), may hold values from -1 to 0, as said below
- ssm_upstream: bfloat16 [1024, 4096], P('ctx', 'grp'), may hold values from -0.59765625 to 0.59765625
Outputs:
- attention_out: bfloat16 [1024, 4096], P('ctx', 'grp')
- queries_grad: bfloat16 [1024, 4096], P('ctx', 'grp')
- keyvalue_grad: bfloat16 [1024, 2, 512], P('ctx', None, 'grp')
- ssm_out: bfloat16 [1024, 4096], P('ctx', 'grp')
- input_grad: bfloat16 [1024, 4096], P('ctx', 'grp')
- write_grad: bfloat16 [1024, 256], P('ctx')
- read_grad: bfloat16 [1024, 256], P('ctx')
Inputs may be any that keep to these rules, and one draw needn't show every extreme that they name: `log_decay`: every entry is below zero.
All inputs are finite; a program needn't handle non-finite values.
Results may differ from a plain program's by a relative error of at most 0.04.
Values may be sent and summed in bfloat16 or wider, within the bound.
A program may use at most 384 MiB of HBM per device.

v0:
```python
import math

import jax
import jax.numpy as jnp
from jax import lax
from jax.sharding import PartitionSpec as P

HEAD_WIDTH = 128
SPAN = 128


HIGH = lax.Precision.HIGHEST


def to_rows(block, groups):
    count = block.shape[0]
    per_group = block.shape[1] // (groups * HEAD_WIDTH)
    return (
        block.reshape(count, groups, per_group, HEAD_WIDTH)
        .transpose(1, 2, 0, 3)
        .reshape(groups, per_group * count, HEAD_WIDTH)
    )


def from_rows(rows_in, count):
    groups = rows_in.shape[0]
    per_group = rows_in.shape[1] // count
    return (
        rows_in.reshape(groups, per_group, count, HEAD_WIDTH)
        .transpose(2, 0, 1, 3)
        .reshape(count, groups * per_group * HEAD_WIDTH)
    )


def key_block(whole, start, length, groups):
    piece = lax.dynamic_slice_in_dim(whole, start, length, 0)
    return (
        piece[:, 0].reshape(length, groups, HEAD_WIDTH),
        piece[:, 1].reshape(length, groups, HEAD_WIDTH),
    )


def masked_scores(query_rows, key_rows, query_pos, key_start, scale):
    length = key_rows.shape[0]
    scores = (
        jnp.einsum("grd,kgd->grk", query_rows, key_rows, preferred_element_type=jnp.float32) * scale
    )
    key_pos = key_start + lax.iota(jnp.int32, length)
    valid = key_pos[None, :] <= query_pos[:, None]
    return jnp.where(valid[None], scores, -jnp.inf)


def attend_grads(
    query_rows, upstream_rows, log_total, row_dots, key_rows, values, query_pos, key_start, scale
):
    scores = masked_scores(query_rows, key_rows, query_pos, key_start, scale)
    exact = jnp.exp(scores - log_total[..., None])
    probs_grad = jnp.einsum(
        "grd,kgd->grk", upstream_rows, values, preferred_element_type=jnp.float32
    )
    scores_grad = (exact * (probs_grad - row_dots[..., None]) * scale).astype(jnp.bfloat16)
    return (exact.astype(jnp.bfloat16), scores_grad)


def pair_grads(scores_grad, probs_low, query_rows, upstream_rows):
    key_part = jnp.einsum(
        "grk,grd->kgd", scores_grad, query_rows, preferred_element_type=jnp.float32
    )
    value_part = jnp.einsum(
        "grk,grd->kgd", probs_low, upstream_rows, preferred_element_type=jnp.float32
    )
    count = key_part.shape[0]
    return jnp.stack((key_part.reshape(count, -1), value_part.reshape(count, -1)), axis=1)


def combine_states(earlier, later):
    return (earlier[0] * later[0], later[0][:, None, None] * earlier[1] + later[1])


def fold_span(acc, item):
    return (combine_states(acc, item), None)


def chain_items(reverse, pieces):
    state_in, growth_in = pieces

    def chain_advance(carry, item):
        acc_growth, acc_state = carry
        item_growth, item_state = item
        return ((acc_growth * item_growth, item_growth * acc_state + item_state), acc_state)

    start = (jnp.ones(growth_in.shape[1:], jnp.float32), jnp.zeros(state_in.shape[1:], jnp.float32))
    return lax.scan(chain_advance, start, (growth_in, state_in), reverse=reverse)[1]


def spread(summary, count):
    heads = summary[0].shape[0]
    flat = summary[1].reshape(1, heads, -1)
    tiled = jnp.broadcast_to(summary[0][None, :, None], (1, heads, count))
    return (flat, tiled)


def block_terms(inputs, writes, reads, decay_log):
    cum_decay = jnp.cumsum(decay_log, axis=1)
    by_head = jnp.transpose(cum_decay, (0, 2, 1))
    length = cum_decay.shape[1]
    lower = lax.iota(jnp.int32, length)[:, None] >= lax.iota(jnp.int32, length)[None, :]
    gaps = by_head[:, :, :, None] - by_head[:, :, None, :]
    decay = jnp.exp(jnp.where(lower, gaps, -jnp.inf))
    gram = jnp.einsum("ctn,csn->cts", reads, writes, precision=HIGH)
    ssm_weights = decay * gram[:, None]
    growth = jnp.exp(cum_decay[:, -1, :])
    tails = jnp.exp(cum_decay[:, -1:, :] - cum_decay)
    heads_in = jnp.exp(cum_decay)
    updates = jnp.einsum("csjp,csn->cjpn", tails[..., None] * inputs, writes, precision=HIGH)
    return (decay, ssm_weights, growth, tails, heads_in, updates)


def block_outputs(inputs, reads, ssm_weights, heads_in, states):
    local = jnp.einsum("cjts,csjp->ctjp", ssm_weights, inputs, precision=HIGH)
    carried = jnp.einsum("cjpn,ctn->ctjp", states, reads, precision=HIGH) * heads_in[..., None]
    return local + carried


def adjoint_terms(upstream, reads, heads_in):
    return jnp.einsum("ctjp,ctn->cjpn", heads_in[..., None] * upstream, reads, precision=HIGH)


def block_grads(
    inputs, writes, reads, upstream, decay, ssm_weights, tails, heads_in, states, adjoints
):
    input_grad = jnp.einsum("cjts,ctjp->csjp", ssm_weights, upstream, precision=HIGH)
    input_grad = input_grad + tails[..., None] * jnp.einsum(
        "cjpn,csn->csjp", adjoints, writes, precision=HIGH
    )
    dots = jnp.einsum("ctjp,csjp->cjts", upstream, inputs, precision=HIGH)
    mixing = jnp.sum(decay * dots, axis=1)
    read_grad = jnp.einsum("cts,csn->ctn", mixing, writes, precision=HIGH)
    read_grad = read_grad + jnp.einsum(
        "cjpn,ctjp->ctn", states, heads_in[..., None] * upstream, precision=HIGH
    )
    write_grad = jnp.einsum("cts,ctn->csn", mixing, reads, precision=HIGH)
    write_grad = write_grad + jnp.einsum(
        "cjpn,csjp->csn", adjoints, tails[..., None] * inputs, precision=HIGH
    )
    return (input_grad, read_grad, write_grad)


def carry_forward(start, growth, updates):

    def carry_advance(state, item):
        return (item[0][:, None, None] * state + item[1], state)

    return lax.scan(carry_advance, start, (growth, updates))[1]


def carry_backward(start, growth, terms):

    def retreat(adjoint, item):
        return (item[0][:, None, None] * adjoint + item[1], adjoint)

    return lax.scan(retreat, start, (growth, terms), reverse=True)[1]


def on_device(
    queries,
    key_value_pair,
    attention_upstream,
    ssm_input,
    write_vec,
    read_vec,
    log_decay,
    ssm_upstream,
):
    rows = queries.shape[0]
    groups = key_value_pair.shape[2] // HEAD_WIDTH
    scale = 1.0 / math.sqrt(HEAD_WIDTH)
    offset = lax.axis_index("ctx") * rows
    whole = lax.all_gather(key_value_pair, "ctx", axis=0, tiled=True)
    total = whole.shape[0]
    block_len = min(512, total)
    count_blocks = (offset + rows - 1) // block_len + 1
    query_rows = to_rows(queries, groups)
    upstream_rows = to_rows(attention_upstream, groups)
    per_group = query_rows.shape[1]
    query_pos = offset + lax.iota(jnp.int32, per_group) % rows

    def gather_stats(index, carry):
        top, norm_sum = carry
        key_rows, values = key_block(whole, index * block_len, block_len, groups)
        scores = masked_scores(query_rows, key_rows, query_pos, index * block_len, scale)
        new_top = jnp.maximum(top, jnp.max(scores, axis=-1))
        norm_sum = norm_sum * jnp.exp(top - new_top) + jnp.sum(
            jnp.exp(scores - new_top[..., None]), axis=-1
        )
        return (new_top, norm_sum)

    start_stats = (
        jnp.full((groups, per_group), -jnp.inf, jnp.float32),
        jnp.zeros((groups, per_group), jnp.float32),
    )
    top, norm_sum = lax.fori_loop(0, count_blocks, gather_stats, start_stats)
    log_total = top + jnp.log(norm_sum)

    def gather_out(index, acc):
        key_rows, values = key_block(whole, index * block_len, block_len, groups)
        scores = masked_scores(query_rows, key_rows, query_pos, index * block_len, scale)
        probs_low = jnp.exp(scores - log_total[..., None]).astype(jnp.bfloat16)
        return acc + jnp.einsum(
            "grk,kgd->grd", probs_low, values, preferred_element_type=jnp.float32
        )

    out_rows = lax.fori_loop(
        0, count_blocks, gather_out, jnp.zeros((groups, per_group, HEAD_WIDTH), jnp.float32)
    )
    out_low = out_rows.astype(jnp.bfloat16)
    attention_out = from_rows(out_low, rows)
    row_dots = jnp.sum(upstream_rows.astype(jnp.float32) * out_low.astype(jnp.float32), axis=-1)
    query_start = jnp.zeros((groups, per_group, HEAD_WIDTH), jnp.float32)

    def step_back(index, carry):
        query_acc, buffer = carry
        start = index * block_len
        key_rows, values = key_block(whole, start, block_len, groups)
        probs_low, scores_grad = attend_grads(
            query_rows,
            upstream_rows,
            log_total,
            row_dots,
            key_rows,
            values,
            query_pos,
            start,
            scale,
        )
        query_acc = query_acc + jnp.einsum(
            "grk,kgd->grd", scores_grad, key_rows, preferred_element_type=jnp.float32
        )
        pair = pair_grads(scores_grad, probs_low, query_rows, upstream_rows)
        return (query_acc, lax.dynamic_update_slice_in_dim(buffer, pair, start, 0))

    buffer_start = jnp.zeros((total, 2, key_value_pair.shape[2]), jnp.float32)
    query_acc, buffer = lax.fori_loop(0, count_blocks, step_back, (query_start, buffer_start))
    pair_total = lax.psum_scatter(buffer, "ctx", scatter_dimension=0, tiled=True)
    queries_grad = from_rows(query_acc.astype(jnp.bfloat16), rows)
    keyvalue_grad = pair_total.astype(jnp.bfloat16)
    heads = log_decay.shape[1]
    span_count = rows // SPAN
    inputs = ssm_input.astype(jnp.float32).reshape(span_count, SPAN, heads, -1)
    writes = write_vec.astype(jnp.float32).reshape(span_count, SPAN, -1)
    reads = read_vec.astype(jnp.float32).reshape(span_count, SPAN, -1)
    decay_log = log_decay.reshape(span_count, SPAN, heads)
    upstream = ssm_upstream.astype(jnp.float32).reshape(span_count, SPAN, heads, -1)
    decay, ssm_weights, growth, tails, heads_in, updates = block_terms(
        inputs, writes, reads, decay_log
    )
    ones = jnp.ones((heads,), jnp.float32)
    zeros = jnp.zeros(updates.shape[1:], jnp.float32)
    summary = lax.scan(fold_span, (ones, zeros), (growth, updates))[0]
    terms = adjoint_terms(upstream, reads, heads_in)
    back_summary = lax.scan(fold_span, (ones, zeros), (growth, terms), reverse=True)[0]
    ctx_count = lax.axis_size("ctx")
    flat, tiled = spread(summary, ctx_count)
    before = chain_items(
        False,
        (
            lax.all_to_all(flat, "ctx", split_axis=2, concat_axis=0, tiled=True),
            lax.all_to_all(tiled, "ctx", split_axis=2, concat_axis=0, tiled=True),
        ),
    )
    start_state = lax.all_to_all(before, "ctx", split_axis=0, concat_axis=2, tiled=True).reshape(
        zeros.shape
    )
    back_flat, back_tiled = spread(back_summary, ctx_count)
    after = chain_items(
        True,
        (
            lax.all_to_all(back_flat, "ctx", split_axis=2, concat_axis=0, tiled=True),
            lax.all_to_all(back_tiled, "ctx", split_axis=2, concat_axis=0, tiled=True),
        ),
    )
    start_adjoint = lax.all_to_all(after, "ctx", split_axis=0, concat_axis=2, tiled=True).reshape(
        zeros.shape
    )
    states = carry_forward(start_state, growth, updates)
    ssm_out = (
        block_outputs(inputs, reads, ssm_weights, heads_in, states)
        .reshape(rows, -1)
        .astype(jnp.bfloat16)
    )
    adjoints = carry_backward(start_adjoint, growth, terms)
    input_grad, read_part, write_part = block_grads(
        inputs, writes, reads, upstream, decay, ssm_weights, tails, heads_in, states, adjoints
    )
    head_total = lax.psum((read_part.reshape(rows, -1), write_part.reshape(rows, -1)), "grp")
    input_grad = input_grad.reshape(rows, -1).astype(jnp.bfloat16)
    write_grad = head_total[1].astype(jnp.bfloat16)
    read_grad = head_total[0].astype(jnp.bfloat16)
    return (attention_out, queries_grad, keyvalue_grad, ssm_out, input_grad, write_grad, read_grad)


def solution(mesh):
    return jax.shard_map(
        on_device,
        mesh=mesh,
        in_specs=(
            P("ctx", "grp"),
            P("ctx", None, "grp"),
            P("ctx", "grp"),
            P("ctx", "grp"),
            P("ctx", None),
            P("ctx", None),
            P("ctx", "grp"),
            P("ctx", "grp"),
        ),
        out_specs=(
            P("ctx", "grp"),
            P("ctx", "grp"),
            P("ctx", None, "grp"),
            P("ctx", "grp"),
            P("ctx", "grp"),
            P("ctx", None),
            P("ctx", None),
        ),
        check_vma=False,
    )
```

profile of v0, /device:TPU:0, one launch (start us, length us, event | category | flops | bytes accessed | tf_op | source)
XLA Modules:
  0.0 453.0 jit_solution(2239567367186582995)
XLA Ops:
  2.3 1.1 copy.100
  3.4 1.2 copy.108
  7.0 1.6 fusion.76
  8.6 1.4 squeeze.43
  10.0 1.2 broadcast_add_fusion
  11.2 12.1 %copy.103 = f32[1,16,16384]{1,0,2:T(1,128)} copy(f32[1,16,16384]{2,1,0:T(8,128)S(1)} %get-tuple-element.578) | data formatting | bytes 2097152 | tf_op jit(solution)/shard_map/while/body/eval_jaxpr/add | solution.py:77
  23.8 74.4 %reduce.7 = f32[16384,16]{1,0:T(8,128)} reduce(f32[16384,1,16]{2,1,0:T(1,128)} %bitcast.337, f32[]{:T(128)} %broadcast.183), dimensions={1}, to_apply=%bitcast.238.reduce_sub_computation | reduce | bytes 2097156
  98.1 8.1 %reshape.409 = f32[8,1,32768]{2,1,0:T(1,128)} reshape(f32[16384,16]{1,0:T(8,128)} %reduce.7) | data formatting | bytes 2097152
  106.2 5.3 %all-to-all-start.1 = ((f32[8,1,32768]{2,1,0:T(1,128)}), f32[8,1,32768]{2,1,0:T(1,128)}, u32[]{:S(2)}, u32[]{:S(2)}) async-start(f32[8,1,32768]{2,1,0:T(1,128)} %reshape.409), calls=%async_computation.1 | async-start | bytes 2097152 | tf_op jit(solution)/shard_map/all_to_all | solution.py:267
  111.6 19.8 %all_gather.3 = bf16[1024,2,128]{2,0,1:T(8,128)(2,1)S(1)} all-gather(bf16[128,2,128]{2,0,1:T(8,128)(2,1)S(1)} %copy.91), channel_id=1, replica_groups=mesh['ctx'=8,'grp'=4] {'ctx'}, dimensions={0}, use_global_device_ids=true | all-gather | bytes 589824 | tf_op jit(solution)/shard_map/all_gather | solution.py:179
  131.5 1.1 while.23
  132.7 1.1 while.88
  132.7 1.0 fusion.129
  135.4 1.2 broadcast_in_dim.92.clone
  136.7 7.9 %while.89 = (s32[]{:T(128)}, f32[1,1024,128]{2,1,0:T(8,128)S(1)}, f32[1024,2,128]{2,1,0:T(2,128)}, s32[]{:T(128)}, bf16[1024,2,128]{2,0,1:T(8,128)(2,1)}, /*inde...) while((s32[]{:T(128)}, f32[1,1024,128]{2,1,0:T(8,128)S(1)}, ...), condition=%wide.region_8.9_spmd.clone, body=%wide.region_7.8_spmd.clone.sunk | while | flops 676077056 | bytes 22958364 | solution.py:243
  137.2 1.5 fusion.138
  138.7 1.3 fusion.139
  143.1 1.4 fusion.140
  145.5 1.8 copy.93
  148.2 12.1 %copy.110 = f32[1,16,16384]{1,0,2:T(1,128)} copy(f32[1,16,16384]{2,1,0:T(8,128)S(1)} %copy-done.6) | data formatting | bytes 2097152 | tf_op jit(solution)/shard_map/while/body/eval_jaxpr/add | solution.py:77
  160.3 74.4 %reduce.9 = f32[16384,16]{1,0:T(8,128)} reduce(f32[16384,1,16]{2,1,0:T(1,128)} %bitcast.338, f32[]{:T(128)} %broadcast.183), dimensions={1}, to_apply=%bitcast.240.reduce_sub_computation | reduce | bytes 2097156
  234.7 8.1 %reshape.411 = f32[8,1,32768]{2,1,0:T(1,128)} reshape(f32[16384,16]{1,0:T(8,128)} %reduce.9) | data formatting | bytes 2097152
  242.9 1.2 fusion.54
  244.1 60.8 %all-reduce.4 = bf16[1024,2,128]{2,1,0:T(2,128)(2,1)} all-reduce(f32[1024,2,128]{2,1,0:T(2,128)S(1)} %copy-done.10), channel_id=2, replica_groups=mesh['ctx'=8,'grp'=4] {'ctx'}, use_global_device_ids=true, to_apply=%region_9.10.clone | all-reduce | flops 262144 | bytes 1572864
  305.5 3.5 all-to-all-start
  310.3 4.3 reduce.8
  314.6 20.6 %reshape.410 = f32[16384,1,16]{2,1,0:T(1,128)} reshape(f32[8,32768]{1,0:T(8,128)S(1)} %reduce.8) | data formatting | bytes 2097152
  335.2 6.0 %copy.106 = f32[8,16,2048]{2,1,0:T(8,128)} copy(f32[8,16,2048]{1,2,0:T(8,128)} %bitcast.339) | data formatting | bytes 2097152
  341.1 4.1 all-to-all-start.3
  345.4 8.4 %while.90 = (s32[]{:T(128)}, f32[16,2048]{1,0:T(8,128)S(1)}, f32[8,16,2048]{2,1,0:T(8,128)S(1)}, f32[8,16,1]{1,2,0:T(1,128)S(1)}, f32[8,16,2048]{2,1,0:T(8,128)}, /*index=5*/s32[]{:T(128)}, s32[]{:T(128)}) while((s32[]{:T(128)}, f32[16,2048]{1,0:T(8,128)S(1)}, f32[8,16,2048]{2,1,0:T(8,128)S(1)}, f32[8,16,1]{1,2,0:T(1,128)S(1)}, ...), condition=%wide.region_12.13_spmd.clone, body=%wide.region_11.12_spmd.clone.sunk | while | flops 131075 | bytes 655652 | solution.py:93
  345.4 1.0 bitcast_add_fusion.4
  353.8 6.9 %all-to-all-done.3 = f32[8,1,32768]{2,1,0:T(1,128)S(1)} async-done(((f32[8,1,32768]{2,1,0:T(1,128)}), f32[8,1,32768]{2,1,0:T(1,128)S(1)}, u32[]{:S(2)}, u32[]{:S(2)}) %all-to-all-start.3) | async-done | bytes 1048608 | tf_op jit(solution)/shard_map/all_to_all | solution.py:278
  360.7 3.6 all-to-all-start.2
  364.2 3.0 reduce.10
  367.3 20.7 %reshape.412 = f32[16384,1,16]{2,1,0:T(1,128)} reshape(f32[8,32768]{1,0:T(8,128)S(1)} %reduce.10) | data formatting | bytes 2097152
  387.9 5.1 %copy.113 = f32[8,16,2048]{2,1,0:T(8,128)S(1)} copy(f32[8,16,2048]{1,2,0:T(8,128)} %bitcast.340) | data formatting | bytes 2097152
  393.0 1.1 broadcast.154.clone.1
  394.1 6.1 %while.91 = (s32[]{:T(128)}, f32[16,2048]{1,0:T(8,128)S(1)}, f32[8,16,2048]{2,1,0:T(8,128)}, f32[8,16,1]{1,2,0:T(1,128)S(1)}, f32[8,16,2048]{2,1,0:T(8,128)S(1)}, /*index=5*/s32[]{:T(128)}, s32[]{:T(128)}, s32[]{:T(128)}) while((s32[]{:T(128)}, f32[16,2048]{1,0:T(8,128)S(1)}, f32[8,16,2048]{2,1,0:T(8,128)}, ...), condition=%wide.region_14.15_spmd.clone, body=%wide.region_13.14_spmd.clone.sunk | while | flops 131076 | bytes 655672 | solution.py:93
  400.3 4.3 all-to-all-start.4
  404.6 1.5 dynamic-slice_convert_fusion
  407.7 1.6 copy.107
  409.3 1.4 reshape.392
  411.4 1.0 convolution_bitcast_fusion.7
  412.5 7.5 %all-to-all-done.4 = f32[8,16,2048]{2,1,0:T(8,128)} async-done(((f32[8,16,2048]{2,1,0:T(8,128)}), f32[8,16,2048]{2,1,0:T(8,128)}, u32[]{:S(2)}, u32[]{:S(2)}) %all-to-all-start.4) | async-done | bytes 1048608 | tf_op jit(solution)/shard_map/all_to_all | solution.py:282
  420.0 1.9 copy.114
  422.1 1.0 convolution_bitcast_fusion.8
  424.3 1.3 fusion.62
  428.2 24.3 %all-reduce.5 = (bf16[128,256]{1,0:T(8,128)(2,1)}, bf16[128,256]{1,0:T(8,128)(2,1)}) all-reduce(f32[128,256]{1,0:T(8,128)S(1)} %convolution_add_fusion.1, f32[128,256]{1,0:T(8,128)S(1)} %convolution_add_fusion), channel_id=1, replica_groups=mesh['ctx'=8,'grp'=4] {'grp'}, use_global_device_ids=true, to_apply=%region_16.17 | all-reduce | flops 65536 | bytes 393216 | tf_op jit(solution)/shard_map/psum | solution.py:295
  (171 shorter events, 32.7 us)
Async XLA Ops:
  0.6 5.6 %copy-start = (bf16[128,256]{1,0:T(8,128)(2,1)S(1)}, bf16[128,256]{1,0:T(8,128)(2,1)}, u32[]{:S(2)}) copy-start(bf16[128,256]{1,0:T(8,128)(2,1)} %param.22) | copy-start | bytes 196612
  1.6 3.1 copy-start.19
  3.4 3.6 copy-start.13
  4.7 238.2 %copy-start.11 = (bf16[128,1024]{0,1:T(8,128)(2,1)}, bf16[128,1024]{0,1:T(8,128)(2,1)S(1)}, u32[]{:S(2)}) copy-start(bf16[128,1024]{0,1:T(8,128)(2,1)S(1)} %copy.108) | copy-start | bytes 786436
  4.7 0.6 copy-start.23
  5.4 0.8 copy-start.2
  5.4 3.2 copy-start.4
  5.5 1.6 copy-start.16
  106.2 5.3 %copy-start.26 = (bf16[128,2,128]{2,1,0:T(2,128)(2,1)S(1)}, bf16[128,2,128]{2,1,0:T(2,128)(2,1)}, u32[]{:S(2)}) copy-start(bf16[128,2,128]{2,1,0:T(2,128)(2,1)} %param.19) | copy-start | bytes 196612
  106.2 25.1 %copy-start.20 = (bf16[128,1024]{1,0:T(8,128)(2,1)S(1)}, bf16[128,1024]{1,0:T(8,128)(2,1)}, u32[]{:S(2)}) copy-start(bf16[128,1024]{1,0:T(8,128)(2,1)} %param.18) | copy-start | bytes 786436
  106.2 198.7 %all-to-all-start.1 = ((f32[8,1,32768]{2,1,0:T(1,128)}), f32[8,1,32768]{2,1,0:T(1,128)}, u32[]{:S(2)}, u32[]{:S(2)}) async-start(f32[8,1,32768]{2,1,0:T(1,128)} %reshape.409), calls=%async_computation.1 | async-start | bytes 2097152 | tf_op jit(solution)/shard_map/all_to_all | solution.py:267
  132.7 1.1 copy-start.21
  133.8 0.8 copy-start.1
  140.5 1.2 copy-start.8
  142.2 1.0 copy-start.9
  144.6 3.7 copy-start.6
  148.2 94.7 %copy-start.29 = (f32[16,128]{1,0:T(8,128)}, f32[16,128]{1,0:T(8,128)S(1)}, u32[]{:S(2)}) copy-start(f32[16,128]{1,0:T(8,128)S(1)} %copy.98) | copy-start | bytes 24580
  234.7 8.2 %copy-start.14 = (bf16[128,1024]{0,1:T(8,128)(2,1)S(1)}, bf16[128,1024]{0,1:T(8,128)(2,1)}, u32[]{:S(2)}) copy-start(bf16[128,1024]{0,1:T(8,128)(2,1)} %copy-done.13) | copy-start | bytes 786436
  242.9 1.2 copy-start.10
  242.9 62.1 %copy-start.31 = (f32[16]{0:T(128)S(1)}, f32[16]{0:T(128)}, u32[]{:S(2)}) copy-start(f32[16]{0:T(128)} %get-tuple-element.574) | copy-start | bytes 196
  242.9 66.2 %copy-start.32 = (u32[32]{0:T(128)S(1)}, u32[32]{0:T(128)}, u32[]{:S(2)}) copy-start(u32[32]{0:T(128)} %constant.174) | copy-start | bytes 388
  242.9 71.7 %copy-start.27 = (pred[128,128]{1,0:T(8,128)(4,1)}, pred[128,128]{1,0:T(8,128)(4,1)S(1)}, u32[]{:S(2)}) copy-start(pred[128,128]{1,0:T(8,128)(4,1)S(1)} %iota_compare_fusion) | copy-start | bytes 49156
  305.5 35.6 %all-to-all-start = ((f32[1,16,8]{1,0,2:T(1,128)}), f32[1,16,8]{1,0,2:T(1,128)S(1)}, u32[]{:S(2)}, u32[]{:S(2)}) async-start(f32[1,16,8]{1,0,2:T(1,128)} %broadcast_in_dim.95), calls=%async_computation | async-start | bytes 8192 | tf_op jit(solution)/shard_map/all_to_all | solution.py:268
  341.1 19.5 %all-to-all-start.3 = ((f32[8,1,32768]{2,1,0:T(1,128)}), f32[8,1,32768]{2,1,0:T(1,128)S(1)}, u32[]{:S(2)}, u32[]{:S(2)}) async-start(f32[8,1,32768]{2,1,0:T(1,128)} %reshape.411), calls=%async_computation.3 | async-start | bytes 2097152 | tf_op jit(solution)/shard_map/all_to_all | solution.py:278
  353.8 6.9 %copy-start.7 = (f32[8,16,2048]{2,1,0:T(8,128)}, f32[8,16,2048]{2,1,0:T(8,128)S(1)}, u32[]{:S(2)}) copy-start(f32[8,16,2048]{2,1,0:T(8,128)S(1)} %get-tuple-element.333) | copy-start | bytes 3145732
  360.7 39.6 %all-to-all-start.2 = ((f32[8,16,2048]{2,1,0:T(8,128)}), f32[8,16,2048]{2,1,0:T(8,128)S(1)}, u32[]{:S(2)}, u32[]{:S(2)}) async-start(f32[8,16,2048]{2,1,0:T(8,128)} %copy-done.7), calls=%async_computation.2 | async-start | bytes 2097152 | tf_op jit(solution)/shard_map/all_to_all | solution.py:271
  394.1 12.7 %copy-start.17 = (bf16[1,8,128,128]{3,1,2,0:T(8,128)(2,1)S(1)}, bf16[1,8,128,128]{3,1,2,0:T(8,128)(2,1)}, u32[]{:S(2)}) copy-start(bf16[1,8,128,128]{3,1,2,0:T(8,128)(2,1)} %copy.95) | copy-start | bytes 786436
  394.1 12.7 %copy-start.18 = (bf16[1,8,128,128]{3,1,2,0:T(8,128)(2,1)S(1)}, bf16[1,8,128,128]{3,1,2,0:T(8,128)(2,1)}, u32[]{:S(2)}) copy-start(bf16[1,8,128,128]{3,1,2,0:T(8,128)(2,1)} %copy.93) | copy-start | bytes 786436
  400.3 19.7 %all-to-all-start.4 = ((f32[8,16,2048]{2,1,0:T(8,128)}), f32[8,16,2048]{2,1,0:T(8,128)}, u32[]{:S(2)}, u32[]{:S(2)}) async-start(f32[8,16,2048]{2,1,0:T(8,128)} %get-tuple-element.334), calls=%async_computation.4 | async-start | bytes 2097152 | tf_op jit(solution)/shard_map/all_to_all | solution.py:282
  407.7 3.0 copy-start.24
  409.3 2.1 copy-start.5
  420.0 2.1 copy-start.3
  422.0 1.7 copy-start.22
  422.1 2.2 copy-start.15
  422.1 2.2 copy-start.25
  422.1 2.2 copy-start.28
  422.1 2.2 copy-start.30
  423.1 3.3 copy-start.12
where the time goes:
time: 462 us; the launch traced here: 453 us
  other arithmetic  174 us (38%)
  local copies, waits for them, and re-layouts  119 us (26%)
  blocking collectives  105 us (23%)
  starting transfers between devices  20.7 us (4%)
  matrix products  16.7 us (4%)
  waiting for transfers between devices  14.4 us (3%)
    unnamed x4, other arithmetic  149 us
    unnamed x77, local copies, waits for them, and re-layouts  76 us
    unnamed x1, blocking collectives  60.8 us
    psum x1, blocking collectives, on_device(): lax.psum((read_part.reshape(rows, -1), write_part.reshape(rows, -1)), 'grp')  24.3 us
    add x2, local copies, waits for them, and re-layouts, combine_states(): later[0][:, None, None] * earlier[1] + later[1]  24.2 us
    all_gather x1, blocking collectives, on_device(): whole = lax.all_gather(key_value_pair, 'ctx', axis=0, tiled=True)  19.8 us
  transfers between devices with their start and end apart: 5, of which 2 were waited for; matrix products, arithmetic and copies ran while one was open for 43% of the time, Pallas kernels for 0%

commit v1 on v0

v1 whole, which is shorter than its diff:
```python
import functools
import math

import jax
import jax.numpy as jnp
from jax import lax
from jax.experimental import pallas as pl
from jax.experimental.pallas import tpu as pltpu
from jax.sharding import PartitionSpec as P

HEAD_WIDTH = 128
MESH = pl.DeviceIdType.MESH
HIGH = lax.Precision.HIGHEST
BF16 = jnp.bfloat16
F32 = jnp.float32


def dot(a, b, ca, cb, precision=None):
    return lax.dot_general(
        a, b, (((ca,), (cb,)), ((), ())), preferred_element_type=F32, precision=precision
    )


def kernel(
    n,
    ng,
    q_ref,
    kv_ref,
    up_ref,
    x_ref,
    wr_ref,
    rd_ref,
    ld_ref,
    su_ref,
    out_ref,
    qg_ref,
    kvg_ref,
    so_ref,
    ig_ref,
    wg_ref,
    rg_ref,
    kv_all,
    tot_all,
    u_own,
    t_own,
    u_sib,
    t_sib,
    u_chip,
    t_chip,
    fw_buf,
    bw_buf,
    s_acc,
    a_acc,
    s_send,
    a_send,
    s_full,
    a_full,
    xs_buf,
    us_buf,
    tails_buf,
    heads_buf,
    rw_acc,
    rs_send,
    rs_buf,
    ag_buf,
    top_buf,
    norm_buf,
    dots_buf,
    outt_buf,
    dqt_buf,
    dkv_send,
    dkv_buf,
    dkv_own,
    kv_s,
    kv_r,
    tot_s,
    tot_r,
    sib_s,
    sib_r,
    fw_s,
    fw_r,
    bw_s,
    bw_r,
    dk_s,
    dk_r,
    rs_s,
    rs_r,
    ag_s,
    ag_r,
):
    rows = q_ref.shape[0]
    heads_q = q_ref.shape[1] // HEAD_WIDTH
    heads = ld_ref.shape[1]
    width = x_ref.shape[1] // heads
    flat = x_ref.shape[1]
    half = flat // 2
    half_heads = heads // 2
    scale = 1.0 / math.sqrt(HEAD_WIDTH)
    chips = n // 2
    me = lax.axis_index("ctx")
    grp = lax.axis_index("grp")
    core = lax.rem(me, 2)
    chip = me // 2
    sib = me + 1 - 2 * core
    part = rows // ng
    my_half = pl.multiple_of(core * half, half)
    sib_half = pl.multiple_of((1 - core) * half, half)
    my_rows = pl.multiple_of(me * rows, rows)

    barrier = pltpu.get_barrier_semaphore()

    def greet(d, _):
        @pl.when(d != me)
        def _():
            pl.semaphore_signal(barrier, inc=1, device_id={"ctx": d}, device_id_type=MESH)

        return 0

    def greet_grp(d, _):
        @pl.when(d != grp)
        def _():
            pl.semaphore_signal(barrier, inc=1, device_id={"grp": d}, device_id_type=MESH)

        return 0

    lax.fori_loop(0, n, greet, 0)
    lax.fori_loop(0, ng, greet_grp, 0)

    def kv_copy(src, dest):
        at = pl.multiple_of(src * rows, rows)
        return pltpu.make_async_remote_copy(
            src_ref=kv_ref,
            dst_ref=kv_all.at[pl.ds(at, rows)],
            send_sem=kv_s.at[dest],
            recv_sem=kv_r.at[src],
            device_id={"ctx": dest},
            device_id_type=MESH,
        )

    def tot_copy(src, dest):
        return pltpu.make_async_remote_copy(
            src_ref=tot_all.at[src],
            dst_ref=tot_all.at[src],
            send_sem=tot_s.at[dest],
            recv_sem=tot_r.at[src],
            device_id={"ctx": dest},
            device_id_type=MESH,
        )

    def sib_copy(src_ref, dst_ref, which):
        return pltpu.make_async_remote_copy(
            src_ref=src_ref,
            dst_ref=dst_ref,
            send_sem=sib_s.at[which],
            recv_sem=sib_r.at[which],
            device_id={"ctx": sib},
            device_id_type=MESH,
        )

    def chip_copy(src_ref, buf, ssem, rsem, src, dest):
        return pltpu.make_async_remote_copy(
            src_ref=src_ref,
            dst_ref=buf.at[src],
            send_sem=ssem.at[dest],
            recv_sem=rsem.at[src],
            device_id={"ctx": 2 * dest + core},
            device_id_type=MESH,
        )

    def dkv_copy(src, dest):
        at = pl.multiple_of(dest * rows, rows)
        return pltpu.make_async_remote_copy(
            src_ref=dkv_send.at[pl.ds(at, rows)],
            dst_ref=dkv_buf.at[src],
            send_sem=dk_s.at[dest],
            recv_sem=dk_r.at[src],
            device_id={"ctx": dest},
            device_id_type=MESH,
        )

    def rs_copy(src, dest):
        at = pl.multiple_of(dest * part, part)
        return pltpu.make_async_remote_copy(
            src_ref=rs_send.at[pl.ds(at, part)],
            dst_ref=rs_buf.at[src],
            send_sem=rs_s.at[dest],
            recv_sem=rs_r.at[src],
            device_id={"grp": dest},
            device_id_type=MESH,
        )

    def ag_copy(src, dest):
        at = pl.multiple_of(src * part, part)
        return pltpu.make_async_remote_copy(
            src_ref=ag_buf.at[pl.ds(at, part)],
            dst_ref=ag_buf.at[pl.ds(at, part)],
            send_sem=ag_s.at[dest],
            recv_sem=ag_r.at[src],
            device_id={"grp": dest},
            device_id_type=MESH,
        )

    def each(low, high, action):
        def body(d, _):
            action(d)
            return 0

        lax.fori_loop(low, high, body, 0)

    decay_log = ld_ref[...]
    row_id = lax.broadcasted_iota(jnp.int32, (rows, rows), 0)
    col_id = lax.broadcasted_iota(jnp.int32, (rows, rows), 1)
    lower = row_id >= col_id
    cum = dot(lower.astype(F32), decay_log, 1, 0, HIGH)
    cum_t = dot(decay_log, (row_id <= col_id).astype(F32), 0, 0, HIGH)
    last = cum[rows - 1 :, :]
    tot = dot(decay_log, jnp.ones((rows, tot_all.shape[2]), F32), 0, 0, HIGH)
    tot_all[me] = tot
    pick = (
        lax.broadcasted_iota(jnp.int32, (heads, flat), 1) // width
        == lax.broadcasted_iota(jnp.int32, (heads, flat), 0)
    ).astype(F32)
    tails = dot(jnp.exp(last - cum), pick, 1, 0, HIGH)
    heads_in = dot(jnp.exp(cum), pick, 1, 0, HIGH)
    tails_buf[...] = tails
    heads_buf[...] = heads_in
    xs_buf[...] = (tails * x_ref[...].astype(F32)).astype(BF16)
    us_buf[...] = (heads_in * su_ref[...].astype(F32)).astype(BF16)
    u_own[...] = dot(xs_buf[...], wr_ref[...], 0, 0).astype(BF16)
    t_own[...] = dot(us_buf[...], rd_ref[...], 0, 0).astype(BF16)

    pl.semaphore_wait(barrier, n - 1 + ng - 1)
    sib_u = sib_copy(u_own.at[pl.ds(sib_half, half)], u_sib, 0)
    sib_t = sib_copy(t_own.at[pl.ds(sib_half, half)], t_sib, 1)
    tot_copy(me, sib).start()
    sib_u.start()
    sib_t.start()

    def send_tot(d):
        @pl.when(d // 2 != chip)
        def _():
            tot_copy(me, d).start()

    each(0, n, send_tot)

    def send_kv(d):
        @pl.when(d != me)
        def _():
            kv_copy(me, d).start()

    each(2 * chip, n, send_kv)
    kv_all[pl.ds(my_rows, rows), :] = kv_ref[...]

    tot_copy(sib, sib).wait_recv()
    sib_u.wait_recv()
    sib_t.wait_recv()
    head_at = pl.multiple_of(core * half_heads, half_heads)
    first = core == 0

    def total_of(device):
        return tot_all[device, pl.ds(head_at, half_heads), :]

    grow_even = jnp.exp(total_of(2 * chip))
    grow_odd = jnp.exp(total_of(2 * chip + 1))

    def pair_of(own, other, h):
        mine = own[pl.ds(pl.multiple_of(my_half + h * width, width), width), :].astype(F32)
        theirs = other[pl.ds(h * width, width), :].astype(F32)
        return jnp.where(first, mine, theirs), jnp.where(first, theirs, mine)

    for h in range(half_heads):
        even, odd = pair_of(u_own, u_sib, h)
        u_chip[h * width : (h + 1) * width, :] = (
            grow_odd[h : h + 1, :] * even + odd
        ).astype(BF16)
        even, odd = pair_of(t_own, t_sib, h)
        t_chip[h * width : (h + 1) * width, :] = (
            even + grow_even[h : h + 1, :] * odd
        ).astype(BF16)

    each(chip + 1, chips, lambda d: chip_copy(u_chip, fw_buf, fw_s, fw_r, chip, d).start())
    each(0, chip, lambda d: chip_copy(t_chip, bw_buf, bw_s, bw_r, chip, d).start())

    gram = dot(rd_ref[...], wr_ref[...], 1, 1)
    gram2 = jnp.concatenate([gram, gram], axis=1)
    lane_low = lax.broadcasted_iota(jnp.int32, (rows, 2 * width), 1) < width
    mixing2 = jnp.zeros((rows, 2 * rows), F32)
    zero = jnp.zeros((rows, 2 * width), BF16)
    for p in range(heads // 2):
        cols = slice(2 * width * p, 2 * width * (p + 1))
        decays = []
        for h in (2 * p, 2 * p + 1):
            gap = cum[:, h : h + 1] - cum_t[h : h + 1, :]
            decays.append(jnp.exp(jnp.where(lower, gap, -jnp.inf)))
        decay = jnp.concatenate(decays, axis=1)
        weights = (decay * gram2).astype(BF16)
        x_pair = x_ref[:, cols]
        x_split = jnp.concatenate(
            [jnp.where(lane_low, x_pair, zero), jnp.where(lane_low, zero, x_pair)], axis=0
        )
        su_pair = su_ref[:, cols]
        mixing2 = mixing2 + decay * dot(su_pair, x_split, 1, 1)
        outt = dot(weights, x_split, 1, 0)
        so_ref[:, cols] = outt.astype(BF16)
        back = dot(weights, su_pair, 0, 0)
        ig_ref[:, cols] = jnp.where(lane_low, back[:rows], back[rows:]).astype(BF16)
    mixing = (mixing2[:, :rows] + mixing2[:, rows:]).astype(BF16)
    n_state = wr_ref.shape[1]
    rw_acc[:, :n_state] = dot(mixing, rd_ref[...], 0, 0)
    rw_acc[:, n_state:] = dot(mixing, wr_ref[...], 1, 0)

    block = 2 * rows
    key_id = lax.broadcasted_iota(jnp.int32, (block, rows), 0)
    query_id = lax.broadcasted_iota(jnp.int32, (block, rows), 1)

    top_buf[...] = jnp.full(top_buf.shape, -jnp.inf, F32)
    norm_buf[...] = jnp.zeros(norm_buf.shape, F32)
    outt_buf[...] = jnp.zeros(outt_buf.shape, F32)

    def forward(j):
        for d in (2 * j, 2 * j + 1):

            @pl.when(d != me)
            def _():
                kv_copy(d, sib).wait_recv()

        at = pl.multiple_of(j * block, block)
        keys = kv_all[pl.ds(at, block), :HEAD_WIDTH]
        values_t = kv_all[pl.ds(at, block), HEAD_WIDTH:].T
        valid = key_id + j * block <= query_id + me * rows
        for h in range(heads_q):
            q = q_ref[:, h * HEAD_WIDTH : (h + 1) * HEAD_WIDTH]
            scores = jnp.where(valid, dot(keys, q, 1, 1) * scale, -jnp.inf)
            top = top_buf[h : h + 1, :]
            new_top = jnp.maximum(top, jnp.max(scores, axis=0, keepdims=True))
            shrink = jnp.exp(top - new_top)
            probs = jnp.exp(scores - new_top)
            norm_buf[h : h + 1, :] = norm_buf[h : h + 1, :] * shrink + jnp.sum(
                probs, axis=0, keepdims=True
            )
            top_buf[h : h + 1, :] = new_top
            outt_buf[h] = outt_buf[h] * shrink + dot(values_t, probs.astype(BF16), 1, 0)

    each(0, chip + 1, forward)

    s_acc[...] = jnp.zeros(s_acc.shape, F32)
    a_acc[...] = jnp.zeros(a_acc.shape, F32)

    def wait_tot(d):
        @pl.when(d // 2 != chip)
        def _():
            tot_copy(d, sib).wait_recv()

    each(0, n, wait_tot)

    def fold(acc, buf, rsem, src_ref, k):
        chip_copy(src_ref, buf, rsem, rsem, k, chip).wait_recv()
        grow = jnp.exp(total_of(2 * k) + total_of(2 * k + 1))
        for h in range(half_heads):
            at = slice(h * width, (h + 1) * width)
            acc[at, :] = grow[h : h + 1, :] * acc[at, :] + buf[k, at, :].astype(F32)

    each(0, chip, lambda k: fold(s_acc, fw_buf, fw_r, u_chip, k))
    each(
        0,
        chips - 1 - chip,
        lambda i: fold(a_acc, bw_buf, bw_r, t_chip, chips - 1 - i),
    )
    for h in range(half_heads):
        at = slice(h * width, (h + 1) * width)
        mine_at = pl.ds(pl.multiple_of(my_half + h * width, width), width)
        even_u, _ = pair_of(u_own, u_sib, h)
        state_even = s_acc[at, :]
        state_odd = grow_even[h : h + 1, :] * state_even + even_u
        s_full[mine_at, :] = jnp.where(first, state_even, state_odd).astype(BF16)
        s_send[at, :] = jnp.where(first, state_odd, state_even).astype(BF16)
        _, odd_t = pair_of(t_own, t_sib, h)
        adj_odd = a_acc[at, :]
        adj_even = grow_odd[h : h + 1, :] * adj_odd + odd_t
        a_full[mine_at, :] = jnp.where(first, adj_even, adj_odd).astype(BF16)
        a_send[at, :] = jnp.where(first, adj_odd, adj_even).astype(BF16)
    back_s = sib_copy(s_send, s_full.at[pl.ds(my_half, half)], 2)
    back_a = sib_copy(a_send, a_full.at[pl.ds(my_half, half)], 3)
    back_s.start()
    back_a.start()

    for h in range(heads_q):
        cols = slice(h * HEAD_WIDTH, (h + 1) * HEAD_WIDTH)
        norm = norm_buf[h : h + 1, :]
        low = (outt_buf[h] / norm).astype(BF16).astype(F32)
        out = low.T
        out_ref[:, cols] = out.astype(BF16)
        up_t = up_ref[:, cols].astype(F32).T
        dots_buf[h : h + 1, :] = jnp.sum(up_t * low, axis=0, keepdims=True)
        top_buf[h : h + 1, :] = top_buf[h : h + 1, :] + jnp.log(norm)
    dqt_buf[...] = jnp.zeros(dqt_buf.shape, F32)

    sib_copy(s_send, s_full.at[pl.ds(sib_half, half)], 2).wait_recv()
    sib_copy(a_send, a_full.at[pl.ds(sib_half, half)], 3).wait_recv()
    rw_acc[:, n_state:] = rw_acc[:, n_state:] + dot(us_buf[...], s_full[...], 1, 0)
    rw_acc[:, :n_state] = rw_acc[:, :n_state] + dot(xs_buf[...], a_full[...], 1, 0)
    rs_send[...] = rw_acc[...].astype(BF16)

    def send_rs(d):
        @pl.when(d != grp)
        def _():
            rs_copy(grp, d).start()

    each(0, ng, send_rs)
    so_ref[...] = (
        so_ref[...].astype(F32) + heads_buf[...] * dot(rd_ref[...], s_full[...], 1, 1)
    ).astype(BF16)
    ig_ref[...] = (
        ig_ref[...].astype(F32) + tails_buf[...] * dot(wr_ref[...], a_full[...], 1, 1)
    ).astype(BF16)

    def backward(j):
        at = pl.multiple_of(j * block, block)
        keys = kv_all[pl.ds(at, block), :HEAD_WIDTH]
        values = kv_all[pl.ds(at, block), HEAD_WIDTH:]
        keys_t = keys.T
        valid = key_id + j * block <= query_id + me * rows
        key_acc = jnp.zeros((block, HEAD_WIDTH), F32)
        value_acc = jnp.zeros((block, HEAD_WIDTH), F32)
        for h in range(heads_q):
            cols = slice(h * HEAD_WIDTH, (h + 1) * HEAD_WIDTH)
            q = q_ref[:, cols]
            up = up_ref[:, cols]
            scores = jnp.where(valid, dot(keys, q, 1, 1) * scale, -jnp.inf)
            exact = jnp.exp(scores - top_buf[h : h + 1, :])
            probs_grad = dot(values, up, 1, 1)
            scores_grad = (exact * (probs_grad - dots_buf[h : h + 1, :]) * scale).astype(BF16)
            dqt_buf[h] = dqt_buf[h] + dot(keys_t, scores_grad, 1, 0)
            key_acc = key_acc + dot(scores_grad, q, 1, 0)
            value_acc = value_acc + dot(exact.astype(BF16), up, 1, 0)
        dkv_send[pl.ds(at, block), :HEAD_WIDTH] = key_acc.astype(BF16)
        dkv_send[pl.ds(at, block), HEAD_WIDTH:] = value_acc.astype(BF16)

        @pl.when(j == chip)
        def _():
            own = core == 0
            dkv_own[:, :HEAD_WIDTH] = jnp.where(own, key_acc[:rows], key_acc[rows:])
            dkv_own[:, HEAD_WIDTH:] = jnp.where(own, value_acc[:rows], value_acc[rows:])

        for d in (2 * j, 2 * j + 1):

            @pl.when(d < me)
            def _():
                dkv_copy(me, d).start()

    each(0, chip + 1, backward)

    total = rw_acc[pl.ds(pl.multiple_of(grp * part, part), part), :]
    rw_acc[pl.ds(0, part), :] = total

    def take_rs(d):
        @pl.when(d != grp)
        def _():
            rs_copy(d, d).wait_recv()
            rw_acc[pl.ds(0, part), :] = rw_acc[pl.ds(0, part), :] + rs_buf[d].astype(F32)

    each(0, ng, take_rs)
    ag_buf[pl.ds(pl.multiple_of(grp * part, part), part), :] = rw_acc[pl.ds(0, part), :].astype(
        BF16
    )

    def send_ag(d):
        @pl.when(d != grp)
        def _():
            ag_copy(grp, d).start()

    each(0, ng, send_ag)

    for h in range(heads_q):
        qg_ref[:, h * HEAD_WIDTH : (h + 1) * HEAD_WIDTH] = dqt_buf[h].T.astype(BF16)

    def take_dkv(d):
        dkv_copy(d, me).wait_recv()
        dkv_own[...] = dkv_own[...] + dkv_buf[d].astype(F32)

    each(me + 1, n, take_dkv)
    kvg_ref[...] = dkv_own[...].astype(BF16)

    def take_ag(d):
        @pl.when(d != grp)
        def _():
            ag_copy(d, d).wait_recv()

    each(0, ng, take_ag)
    wg_ref[...] = ag_buf[:, :n_state]
    rg_ref[...] = ag_buf[:, n_state:]

    def end_ctx(d):
        @pl.when(d != me)
        def _():
            tot_copy(me, d).wait_send()

            @pl.when(d >= 2 * chip)
            def _():
                kv_copy(me, d).wait_send()

            @pl.when(d < me)
            def _():
                dkv_copy(me, d).wait_send()

    each(0, n, end_ctx)
    sib_u.wait_send()
    sib_t.wait_send()
    back_s.wait_send()
    back_a.wait_send()
    each(chip + 1, chips, lambda d: chip_copy(u_chip, fw_buf, fw_s, fw_r, chip, d).wait_send())
    each(0, chip, lambda d: chip_copy(t_chip, bw_buf, bw_s, bw_r, chip, d).wait_send())

    def end_grp(d):
        @pl.when(d != grp)
        def _():
            rs_copy(grp, d).wait_send()
            ag_copy(grp, d).wait_send()

    each(0, ng, end_grp)


def on_device(
    queries,
    key_value_pair,
    attention_upstream,
    ssm_input,
    write_vec,
    read_vec,
    log_decay,
    ssm_upstream,
):
    n = lax.axis_size("ctx")
    ng = lax.axis_size("grp")
    rows, cols = queries.shape
    heads_q = cols // HEAD_WIDTH
    flat = ssm_input.shape[1]
    heads = log_decay.shape[1]
    n_state = write_vec.shape[1]
    chips = n // 2
    half = flat // 2
    pair = key_value_pair.reshape(rows, 2 * HEAD_WIDTH)
    vm = pltpu.VMEM
    dma = pltpu.SemaphoreType.DMA
    outs = pl.pallas_call(
        functools.partial(kernel, n, ng),
        out_shape=(
            jax.ShapeDtypeStruct((rows, cols), BF16),
            jax.ShapeDtypeStruct((rows, cols), BF16),
            jax.ShapeDtypeStruct((rows, 2 * HEAD_WIDTH), BF16),
            jax.ShapeDtypeStruct((rows, flat), BF16),
            jax.ShapeDtypeStruct((rows, flat), BF16),
            jax.ShapeDtypeStruct((rows, n_state), BF16),
            jax.ShapeDtypeStruct((rows, n_state), BF16),
        ),
        in_specs=[pl.BlockSpec(memory_space=pltpu.VMEM)] * 8,
        out_specs=[pl.BlockSpec(memory_space=pltpu.VMEM)] * 7,
        scratch_shapes=[
            vm((n * rows, 2 * HEAD_WIDTH), BF16),
            vm((n, heads, n_state), F32),
            vm((flat, n_state), BF16),
            vm((flat, n_state), BF16),
            vm((half, n_state), BF16),
            vm((half, n_state), BF16),
            vm((half, n_state), BF16),
            vm((half, n_state), BF16),
            vm((chips, half, n_state), BF16),
            vm((chips, half, n_state), BF16),
            vm((half, n_state), F32),
            vm((half, n_state), F32),
            vm((half, n_state), BF16),
            vm((half, n_state), BF16),
            vm((flat, n_state), BF16),
            vm((flat, n_state), BF16),
            vm((rows, flat), BF16),
            vm((rows, flat), BF16),
            vm((rows, flat), F32),
            vm((rows, flat), F32),
            vm((rows, 2 * n_state), F32),
            vm((rows, 2 * n_state), BF16),
            vm((ng, rows // ng, 2 * n_state), BF16),
            vm((rows, 2 * n_state), BF16),
            vm((heads_q, rows), F32),
            vm((heads_q, rows), F32),
            vm((heads_q, rows), F32),
            vm((heads_q, HEAD_WIDTH, rows), F32),
            vm((heads_q, HEAD_WIDTH, rows), F32),
            vm((n * rows, 2 * HEAD_WIDTH), BF16),
            vm((n, rows, 2 * HEAD_WIDTH), BF16),
            vm((rows, 2 * HEAD_WIDTH), F32),
            dma((n,)),
            dma((n,)),
            dma((n,)),
            dma((n,)),
            dma((4,)),
            dma((4,)),
            dma((chips,)),
            dma((chips,)),
            dma((chips,)),
            dma((chips,)),
            dma((n,)),
            dma((n,)),
            dma((ng,)),
            dma((ng,)),
            dma((ng,)),
            dma((ng,)),
        ],
        compiler_params=pltpu.CompilerParams(
            collective_id=0, has_side_effects=True, vmem_limit_bytes=56 * 1024 * 1024
        ),
    )(
        queries,
        pair,
        attention_upstream,
        ssm_input,
        write_vec,
        read_vec,
        log_decay,
        ssm_upstream,
    )
    out, qg, kvg, so, ig, wg, rg = outs
    return (out, qg, kvg.reshape(rows, 2, HEAD_WIDTH), so, ig, wg, rg)


def solution(mesh):
    return jax.shard_map(
        on_device,
        mesh=mesh,
        in_specs=(
            P("ctx", "grp"),
            P("ctx", None, "grp"),
            P("ctx", "grp"),
            P("ctx", "grp"),
            P("ctx", None),
            P("ctx", None),
            P("ctx", "grp"),
            P("ctx", "grp"),
        ),
        out_specs=(
            P("ctx", "grp"),
            P("ctx", "grp"),
            P("ctx", None, "grp"),
            P("ctx", "grp"),
            P("ctx", "grp"),
            P("ctx", None),
            P("ctx", None),
        ),
        check_vma=False,
    )
```

time: 462 us -> 53 us (0.11)
  the two profiles are of different devices: /device:TPU:0 before, /device:TPU:7 now
where the time goes in v1:
time: 53 us; the launch traced here: 52.6 us
  Pallas kernels  42.1 us (79%)
  local copies, waits for them, and re-layouts  9.86 us (19%)
  between operations  0.66 us (1%)
    pallas_call x1, Pallas kernels, on_device(): pl.pallas_call(functools.partial(kernel, n, ng), out_shape=(jax.ShapeDtyp...  42.1 us
    unnamed x20, local copies, waits for them, and re-layouts  8.37 us
    reshape x1, local copies, waits for them, and re-layouts, on_device(): return (out, qg, kvg.reshape(rows, 2, HEAD_WIDTH), so, ig, wg, rg)  1.49 us

profile of v1, /device:TPU:7, one launch (start us, length us, event | category | flops | bytes accessed | tf_op | source)
XLA Modules:
  0.0 52.6 jit_solution(6271484590146564790)
XLA Ops:
  0.6 0.0 copy-start.5
  0.6 1.5 %copy.18 = bf16[16,8,2,128]{3,1,2,0:T(8,128)(2,1)} copy(bf16[16,8,2,128]{3,2,1,0:T(2,128)(2,1)} %bitcast.5) | data formatting | bytes 131072
  2.1 0.0 copy-done.5
  2.1 0.7 %copy.15.ld_ref = f32[128,16]{1,0:T(8,128)} copy(f32[128,16]{0,1:T(8,128)S(1)} %copy-done.5) | data formatting | bytes 16384 | tf_op args[6]
  2.9 42.1 %shard_map.135 = (bf16[128,1024]{1,0:T(8,128)(2,1)}, bf16[128,1024]{1,0:T(8,128)(2,1)}, bf16[128,256]{1,0:T(8,128)(2,1)}, bf16[128,1024]{1,0:T(8,128)(2,1)}, bf1...) custom-call(bf16[128,1024]{1,0:T(8,128)(2,1)} %q_ref.1, bf16[128,256]{1,0:T(8,128)(2,1)} %bitcast.4, ...), custom_call_target="tpu_custom_call" | custom-call | tf_op jit(solution)/shard_map/pallas_call | solution.py:545
  45.0 1.5 %reshape.21 = bf16[128,2,128]{2,1,0:T(2,128)(2,1)} reshape(bf16[128,256]{1,0:T(8,128)(2,1)} %get-tuple-element.16) | data formatting | bytes 131072 | tf_op jit(solution)/shard_map/reshape | solution.py:622
  46.5 0.0 copy-start.2
  46.5 1.7 %copy.25 = bf16[128,1024]{1,0:T(8,128)(2,1)} copy(bf16[128,1024]{1,0:T(8,128)(2,1)} %get-tuple-element.28) | data formatting | bytes 524288
  48.2 0.0 copy-done.2
  48.2 0.0 copy-start.1
  48.2 0.7 %copy.26 = bf16[128,1024]{1,0:T(8,128)(2,1)} copy(bf16[128,1024]{1,0:T(8,128)(2,1)S(1)} %copy-done.2) | data formatting | bytes 524288
  48.9 0.3 copy-done.1
  49.2 0.0 copy-start
  49.2 0.7 %copy.27 = bf16[128,1024]{1,0:T(8,128)(2,1)} copy(bf16[128,1024]{1,0:T(8,128)(2,1)S(1)} %copy-done.1) | data formatting | bytes 524288
  49.9 0.3 copy-done
  50.3 0.0 copy-start.4
  50.3 0.7 %copy.28 = bf16[128,1024]{1,0:T(8,128)(2,1)} copy(bf16[128,1024]{1,0:T(8,128)(2,1)S(1)} %copy-done) | data formatting | bytes 524288
  51.0 0.2 copy-done.4
  51.1 0.0 copy-start.3
  51.1 0.6 %copy.29 = bf16[128,256]{1,0:T(8,128)(2,1)} copy(bf16[128,256]{1,0:T(8,128)(2,1)S(1)} %copy-done.4) | data formatting | bytes 131072
  51.8 0.2 copy-done.3
  52.0 0.6 %copy.30 = bf16[128,256]{1,0:T(8,128)(2,1)} copy(bf16[128,256]{1,0:T(8,128)(2,1)S(1)} %copy-done.3) | data formatting | bytes 131072
Async XLA Ops:
  0.6 1.5 %copy-start.5 = (f32[128,16]{0,1:T(8,128)S(1)}, f32[128,16]{0,1:T(8,128)}, u32[]{:S(2)}) copy-start(f32[128,16]{0,1:T(8,128)} %param.14) | copy-start | bytes 24580
  46.5 1.7 %copy-start.2 = (bf16[128,1024]{1,0:T(8,128)(2,1)S(1)}, bf16[128,1024]{1,0:T(8,128)(2,1)}, u32[]{:S(2)}) copy-start(bf16[128,1024]{1,0:T(8,128)(2,1)} %get-tuple-element.29) | copy-start | bytes 786436
  48.2 1.0 %copy-start.1 = (bf16[128,1024]{1,0:T(8,128)(2,1)S(1)}, bf16[128,1024]{1,0:T(8,128)(2,1)}, u32[]{:S(2)}) copy-start(bf16[128,1024]{1,0:T(8,128)(2,1)} %get-tuple-element.31) | copy-start | bytes 786436
  49.2 1.0 %copy-start = (bf16[128,1024]{1,0:T(8,128)(2,1)S(1)}, bf16[128,1024]{1,0:T(8,128)(2,1)}, u32[]{:S(2)}) copy-start(bf16[128,1024]{1,0:T(8,128)(2,1)} %get-tuple-element.32) | copy-start | bytes 786436
  50.3 0.9 %copy-start.4 = (bf16[128,256]{1,0:T(8,128)(2,1)S(1)}, bf16[128,256]{1,0:T(8,128)(2,1)}, u32[]{:S(2)}) copy-start(bf16[128,256]{1,0:T(8,128)(2,1)} %get-tuple-element.33) | copy-start | bytes 196612
  51.1 0.9 %copy-start.3 = (bf16[128,256]{1,0:T(8,128)(2,1)S(1)}, bf16[128,256]{1,0:T(8,128)(2,1)}, u32[]{:S(2)}) copy-start(bf16[128,256]{1,0:T(8,128)(2,1)} %get-tuple-element.34) | copy-start | bytes 196612

commit v2 on v1

--- a/solution.py
+++ b/solution.py
@@ -90,7 +90,7 @@
 ):
     rows = q_ref.shape[0]
     heads_q = q_ref.shape[1] // HEAD_WIDTH
-    heads = ld_ref.shape[1]
+    heads = ld_ref.shape[0]
     width = x_ref.shape[1] // heads
     flat = x_ref.shape[1]
     half = flat // 2
@@ -129,7 +129,7 @@
     def kv_copy(src, dest):
         at = pl.multiple_of(src * rows, rows)
         return pltpu.make_async_remote_copy(
-            src_ref=kv_ref,
+            src_ref=kv_all.at[pl.ds(at, rows)],
             dst_ref=kv_all.at[pl.ds(at, rows)],
             send_sem=kv_s.at[dest],
             recv_sem=kv_r.at[src],
@@ -211,11 +211,10 @@
     row_id = lax.broadcasted_iota(jnp.int32, (rows, rows), 0)
     col_id = lax.broadcasted_iota(jnp.int32, (rows, rows), 1)
     lower = row_id >= col_id
-    cum = dot(lower.astype(F32), decay_log, 1, 0, HIGH)
-    cum_t = dot(decay_log, (row_id <= col_id).astype(F32), 0, 0, HIGH)
+    cum = dot(lower.astype(F32), decay_log, 1, 1, HIGH)
+    cum_t = dot(decay_log, (row_id <= col_id).astype(F32), 1, 0, HIGH)
     last = cum[rows - 1 :, :]
-    tot = dot(decay_log, jnp.ones((rows, tot_all.shape[2]), F32), 0, 0, HIGH)
-    tot_all[me] = tot
+    tot_all[me] = jnp.broadcast_to(cum_t[:, rows - 1 :], tot_all.shape[1:])
     pick = (
         lax.broadcasted_iota(jnp.int32, (heads, flat), 1) // width
         == lax.broadcasted_iota(jnp.int32, (heads, flat), 0)
@@ -229,6 +228,9 @@
     u_own[...] = dot(xs_buf[...], wr_ref[...], 0, 0).astype(BF16)
     t_own[...] = dot(us_buf[...], rd_ref[...], 0, 0).astype(BF16)
 
+    kv_all[pl.ds(my_rows, rows), :HEAD_WIDTH] = kv_ref[:, 0, :]
+    kv_all[pl.ds(my_rows, rows), HEAD_WIDTH:] = kv_ref[:, 1, :]
+
     pl.semaphore_wait(barrier, n - 1 + ng - 1)
     sib_u = sib_copy(u_own.at[pl.ds(sib_half, half)], u_sib, 0)
     sib_t = sib_copy(t_own.at[pl.ds(sib_half, half)], t_sib, 1)
@@ -249,7 +251,6 @@
             kv_copy(me, d).start()
 
     each(2 * chip, n, send_kv)
-    kv_all[pl.ds(my_rows, rows), :] = kv_ref[...]
 
     tot_copy(sib, sib).wait_recv()
     sib_u.wait_recv()
@@ -342,6 +343,53 @@
             outt_buf[h] = outt_buf[h] * shrink + dot(values_t, probs.astype(BF16), 1, 0)
 
     each(0, chip + 1, forward)
+
+    for h in range(heads_q):
+        cols = slice(h * HEAD_WIDTH, (h + 1) * HEAD_WIDTH)
+        norm = norm_buf[h : h + 1, :]
+        low = (outt_buf[h] / norm).astype(BF16).astype(F32)
+        out = low.T
+        out_ref[:, cols] = out.astype(BF16)
+        up_t = up_ref[:, cols].astype(F32).T
+        dots_buf[h : h + 1, :] = jnp.sum(up_t * low, axis=0, keepdims=True)
+        top_buf[h : h + 1, :] = top_buf[h : h + 1, :] + jnp.log(norm)
+    dqt_buf[...] = jnp.zeros(dqt_buf.shape, F32)
+
+    def backward(j):
+        at = pl.multiple_of(j * block, block)
+        keys = kv_all[pl.ds(at, block), :HEAD_WIDTH]
+        values = kv_all[pl.ds(at, block), HEAD_WIDTH:]
+        keys_t = keys.T
+        valid = key_id + j * block <= query_id + me * rows
+        key_acc = jnp.zeros((block, HEAD_WIDTH), F32)
+        value_acc = jnp.zeros((block, HEAD_WIDTH), F32)
+        for h in range(heads_q):
+            cols = slice(h * HEAD_WIDTH, (h + 1) * HEAD_WIDTH)
+            q = q_ref[:, cols]
+            up = up_ref[:, cols]
+            scores = jnp.where(valid, dot(keys, q, 1, 1) * scale, -jnp.inf)
+            exact = jnp.exp(scores - top_buf[h : h + 1, :])
+            probs_grad = dot(values, up, 1, 1)
+            scores_grad = (exact * (probs_grad - dots_buf[h : h + 1, :]) * scale).astype(BF16)
+            dqt_buf[h] = dqt_buf[h] + dot(keys_t, scores_grad, 1, 0)
+            key_acc = key_acc + dot(scores_grad, q, 1, 0)
+            value_acc = value_acc + dot(exact.astype(BF16), up, 1, 0)
+        dkv_send[pl.ds(at, block), :HEAD_WIDTH] = key_acc.astype(BF16)
+        dkv_send[pl.ds(at, block), HEAD_WIDTH:] = value_acc.astype(BF16)
+
+        @pl.when(j == chip)
+        def _():
+            own = core == 0
+            dkv_own[:, :HEAD_WIDTH] = jnp.where(own, key_acc[:rows], key_acc[rows:])
+            dkv_own[:, HEAD_WIDTH:] = jnp.where(own, value_acc[:rows], value_acc[rows:])
+
+        for d in (2 * j, 2 * j + 1):
+
+            @pl.when(d < me)
+            def _():
+                dkv_copy(me, d).start()
+
+    each(0, chip + 1, backward)
 
     s_acc[...] = jnp.zeros(s_acc.shape, F32)
     a_acc[...] = jnp.zeros(a_acc.shape, F32)
@@ -384,17 +432,6 @@
     back_s.start()
     back_a.start()
 
-    for h in range(heads_q):
-        cols = slice(h * HEAD_WIDTH, (h + 1) * HEAD_WIDTH)
-        norm = norm_buf[h : h + 1, :]
-        low = (outt_buf[h] / norm).astype(BF16).astype(F32)
-        out = low.T
-        out_ref[:, cols] = out.astype(BF16)
-        up_t = up_ref[:, cols].astype(F32).T
-        dots_buf[h : h + 1, :] = jnp.sum(up_t * low, axis=0, keepdims=True)
-        top_buf[h : h + 1, :] = top_buf[h : h + 1, :] + jnp.log(norm)
-    dqt_buf[...] = jnp.zeros(dqt_buf.shape, F32)
-
     sib_copy(s_send, s_full.at[pl.ds(sib_half, half)], 2).wait_recv()
     sib_copy(a_send, a_full.at[pl.ds(sib_half, half)], 3).wait_recv()
     rw_acc[:, n_state:] = rw_acc[:, n_state:] + dot(us_buf[...], s_full[...], 1, 0)
@@ -414,42 +451,6 @@
         ig_ref[...].astype(F32) + tails_buf[...] * dot(wr_ref[...], a_full[...], 1, 1)
     ).astype(BF16)
 
-    def backward(j):
-        at = pl.multiple_of(j * block, block)
-        keys = kv_all[pl.ds(at, block), :HEAD_WIDTH]
-        values = kv_all[pl.ds(at, block), HEAD_WIDTH:]
-        keys_t = keys.T
-        valid = key_id + j * block <= query_id + me * rows
-        key_acc = jnp.zeros((block, HEAD_WIDTH), F32)
-        value_acc = jnp.zeros((block, HEAD_WIDTH), F32)
-        for h in range(heads_q):
-            cols = slice(h * HEAD_WIDTH, (h + 1) * HEAD_WIDTH)
-            q = q_ref[:, cols]
-            up = up_ref[:, cols]
-            scores = jnp.where(valid, dot(keys, q, 1, 1) * scale, -jnp.inf)
-            exact = jnp.exp(scores - top_buf[h : h + 1, :])
-            probs_grad = dot(values, up, 1, 1)
-            scores_grad = (exact * (probs_grad - dots_buf[h : h + 1, :]) * scale).astype(BF16)
-            dqt_buf[h] = dqt_buf[h] + dot(keys_t, scores_grad, 1, 0)
-            key_acc = key_acc + dot(scores_grad, q, 1, 0)
-            value_acc = value_acc + dot(exact.astype(BF16), up, 1, 0)
-        dkv_send[pl.ds(at, block), :HEAD_WIDTH] = key_acc.astype(BF16)
-        dkv_send[pl.ds(at, block), HEAD_WIDTH:] = value_acc.astype(BF16)
-
-        @pl.when(j == chip)
-        def _():
-            own = core == 0
-            dkv_own[:, :HEAD_WIDTH] = jnp.where(own, key_acc[:rows], key_acc[rows:])
-            dkv_own[:, HEAD_WIDTH:] = jnp.where(own, value_acc[:rows], value_acc[rows:])
-
-        for d in (2 * j, 2 * j + 1):
-
-            @pl.when(d < me)
-            def _():
-                dkv_copy(me, d).start()
-
-    each(0, chip + 1, backward)
-
     total = rw_acc[pl.ds(pl.multiple_of(grp * part, part), part), :]
     rw_acc[pl.ds(0, part), :] = total
 
@@ -518,6 +519,16 @@
             ag_copy(grp, d).wait_send()
 
     each(0, ng, end_grp)
+
+
+def store(*refs):
+    for index in range(7):
+        source, target = refs[index], refs[7 + index]
+        if index == 2:
+            target[:, 0, :] = source[:, :HEAD_WIDTH]
+            target[:, 1, :] = source[:, HEAD_WIDTH:]
+        else:
+            target[...] = source[...]
 
 
 def on_device(
@@ -539,7 +550,6 @@
     n_state = write_vec.shape[1]
     chips = n // 2
     half = flat // 2
-    pair = key_value_pair.reshape(rows, 2 * HEAD_WIDTH)
     vm = pltpu.VMEM
     dma = pltpu.SemaphoreType.DMA
     outs = pl.pallas_call(
@@ -610,16 +620,28 @@
         ),
     )(
         queries,
-        pair,
+        key_value_pair,
         attention_upstream,
         ssm_input,
         write_vec,
         read_vec,
-        log_decay,
+        log_decay.T,
         ssm_upstream,
     )
-    out, qg, kvg, so, ig, wg, rg = outs
-    return (out, qg, kvg.reshape(rows, 2, HEAD_WIDTH), so, ig, wg, rg)
+    return pl.pallas_call(
+        store,
+        out_shape=(
+            jax.ShapeDtypeStruct((rows, cols), BF16),
+            jax.ShapeDtypeStruct((rows, cols), BF16),
+            jax.ShapeDtypeStruct((rows, 2, HEAD_WIDTH), BF16),
+            jax.ShapeDtypeStruct((rows, flat), BF16),
+            jax.ShapeDtypeStruct((rows, flat), BF16),
+            jax.ShapeDtypeStruct((rows, n_state), BF16),
+            jax.ShapeDtypeStruct((rows, n_state), BF16),
+        ),
+        in_specs=[pl.BlockSpec(memory_space=pltpu.VMEM)] * 7,
+        out_specs=[pl.BlockSpec(memory_space=pltpu.VMEM)] * 7,
+    )(*outs)
 
 
 def solution(mesh):

time: 53 us -> 44.4 us (0.84)
  the two profiles are of different devices: /device:TPU:7 before, /device:TPU:4 now
where the time goes in v2:
time: 44.4 us; the launch traced here: 44.3 us
  Pallas kernels  43.6 us (98%)
  between operations  0.64 us (1%)
    pallas_call x1, Pallas kernels, on_device(): pl.pallas_call(functools.partial(kernel, n, ng), out_shape=(jax.ShapeDtyp...  41.3 us
    pallas_call x1, Pallas kernels, on_device(): pl.pallas_call(store, out_shape=(jax.ShapeDtypeStruct((rows, cols), BF16)...  2.27 us

profile of v2, /device:TPU:4, one launch (start us, length us, event | category | flops | bytes accessed | tf_op | source)
XLA Modules:
  0.0 44.3 jit_solution(2603550753379735731)
XLA Ops:
  0.6 41.3 %shard_map.135 = (bf16[128,1024]{1,0:T(8,128)(2,1)}, bf16[128,1024]{1,0:T(8,128)(2,1)}, bf16[128,256]{1,0:T(8,128)(2,1)}, bf16[128,1024]{1,0:T(8,128)(2,1)}, bf1...) custom-call(bf16[128,1024]{1,0:T(8,128)(2,1)} %q_ref.1, bf16[128,2,128]{2,1,0:T(2,128)(2,1)} %kv_ref.1, ...), custom_call_target="tpu_custom_call" | custom-call | tf_op jit(solution)/shard_map/pallas_call | solution.py:555
  42.0 2.3 %shard_map.136 = (bf16[128,1024]{1,0:T(8,128)(2,1)}, bf16[128,1024]{1,0:T(8,128)(2,1)}, bf16[128,2,128]{2,1,0:T(2,128)(2,1)}, bf16[128,1024]{1,0:T(8,128)(2,1)},...) custom-call(bf16[128,1024]{1,0:T(8,128)(2,1)} %get-tuple-element.14.refs_0_, ...), custom_call_target="tpu_custom_call" | custom-call | tf_op jit(solution)/shard_map/pallas_call | solution.py:631

commit v3 on v2

--- a/solution.py
+++ b/solution.py
@@ -11,6 +11,7 @@
 HEAD_WIDTH = 128
 MESH = pl.DeviceIdType.MESH
 HIGH = lax.Precision.HIGHEST
+PIECES = 2
 BF16 = jnp.bfloat16
 F32 = jnp.float32
 
@@ -103,6 +104,8 @@
     chip = me // 2
     sib = me + 1 - 2 * core
     part = rows // ng
+    heads_piece = half_heads // PIECES
+    piece = heads_piece * width
     my_half = pl.multiple_of(core * half, half)
     sib_half = pl.multiple_of((1 - core) * half, half)
     my_rows = pl.multiple_of(me * rows, rows)
@@ -126,12 +129,12 @@
     lax.fori_loop(0, n, greet, 0)
     lax.fori_loop(0, ng, greet_grp, 0)
 
-    def kv_copy(src, dest):
+    def kv_copy(src, dest, send=None):
         at = pl.multiple_of(src * rows, rows)
         return pltpu.make_async_remote_copy(
             src_ref=kv_all.at[pl.ds(at, rows)],
             dst_ref=kv_all.at[pl.ds(at, rows)],
-            send_sem=kv_s.at[dest],
+            send_sem=kv_s.at[dest if send is None else send],
             recv_sem=kv_r.at[src],
             device_id={"ctx": dest},
             device_id_type=MESH,
@@ -157,12 +160,13 @@
             device_id_type=MESH,
         )
 
-    def chip_copy(src_ref, buf, ssem, rsem, src, dest):
+    def chip_copy(src_ref, buf, ssem, rsem, src, dest, part_at):
+        span = pl.ds(part_at * piece, piece)
         return pltpu.make_async_remote_copy(
-            src_ref=src_ref,
-            dst_ref=buf.at[src],
-            send_sem=ssem.at[dest],
-            recv_sem=rsem.at[src],
+            src_ref=src_ref.at[span],
+            dst_ref=buf.at[src, span],
+            send_sem=ssem.at[dest, part_at],
+            recv_sem=rsem.at[src, part_at],
             device_id={"ctx": 2 * dest + core},
             device_id_type=MESH,
         )
@@ -232,11 +236,20 @@
     kv_all[pl.ds(my_rows, rows), HEAD_WIDTH:] = kv_ref[:, 1, :]
 
     pl.semaphore_wait(barrier, n - 1 + ng - 1)
-    sib_u = sib_copy(u_own.at[pl.ds(sib_half, half)], u_sib, 0)
-    sib_t = sib_copy(t_own.at[pl.ds(sib_half, half)], t_sib, 1)
     tot_copy(me, sib).start()
-    sib_u.start()
-    sib_t.start()
+
+    def part_rows(base, i):
+        return pl.ds(pl.multiple_of(base + i * piece, piece), piece)
+
+    def sib_pieces(i):
+        return (
+            sib_copy(u_own.at[part_rows(sib_half, i)], u_sib.at[pl.ds(i * piece, piece)], 4 * i),
+            sib_copy(t_own.at[part_rows(sib_half, i)], t_sib.at[pl.ds(i * piece, piece)], 4 * i + 1),
+        )
+
+    for i in range(PIECES):
+        for copy in sib_pieces(i):
+            copy.start()
 
     def send_tot(d):
         @pl.when(d // 2 != chip)
@@ -245,16 +258,10 @@
 
     each(0, n, send_tot)
 
-    def send_kv(d):
-        @pl.when(d != me)
-        def _():
-            kv_copy(me, d).start()
-
-    each(2 * chip, n, send_kv)
+    kv_copy(me, sib).start()
+    each(chip + 1, chips, lambda k: kv_copy(me, 2 * k + core).start())
 
     tot_copy(sib, sib).wait_recv()
-    sib_u.wait_recv()
-    sib_t.wait_recv()
     head_at = pl.multiple_of(core * half_heads, half_heads)
     first = core == 0
 
@@ -269,18 +276,20 @@
         theirs = other[pl.ds(h * width, width), :].astype(F32)
         return jnp.where(first, mine, theirs), jnp.where(first, theirs, mine)
 
-    for h in range(half_heads):
-        even, odd = pair_of(u_own, u_sib, h)
-        u_chip[h * width : (h + 1) * width, :] = (
-            grow_odd[h : h + 1, :] * even + odd
-        ).astype(BF16)
-        even, odd = pair_of(t_own, t_sib, h)
-        t_chip[h * width : (h + 1) * width, :] = (
-            even + grow_even[h : h + 1, :] * odd
-        ).astype(BF16)
-
-    each(chip + 1, chips, lambda d: chip_copy(u_chip, fw_buf, fw_s, fw_r, chip, d).start())
-    each(0, chip, lambda d: chip_copy(t_chip, bw_buf, bw_s, bw_r, chip, d).start())
+    for i in range(PIECES):
+        for copy in sib_pieces(i):
+            copy.wait_recv()
+        for h in range(i * heads_piece, (i + 1) * heads_piece):
+            even, odd = pair_of(u_own, u_sib, h)
+            u_chip[h * width : (h + 1) * width, :] = (
+                grow_odd[h : h + 1, :] * even + odd
+            ).astype(BF16)
+            even, odd = pair_of(t_own, t_sib, h)
+            t_chip[h * width : (h + 1) * width, :] = (
+                even + grow_even[h : h + 1, :] * odd
+            ).astype(BF16)
+        each(chip + 1, chips, lambda d: chip_copy(u_chip, fw_buf, fw_s, fw_r, chip, d, i).start())
+        each(0, chip, lambda d: chip_copy(t_chip, bw_buf, bw_s, bw_r, chip, d, i).start())
 
     gram = dot(rd_ref[...], wr_ref[...], 1, 1)
     gram2 = jnp.concatenate([gram, gram], axis=1)
@@ -314,17 +323,18 @@
     key_id = lax.broadcasted_iota(jnp.int32, (block, rows), 0)
     query_id = lax.broadcasted_iota(jnp.int32, (block, rows), 1)
 
+    def relay(k):
+        kv_copy(2 * k + core, me).wait_recv()
+        kv_copy(2 * k + core, sib, 2 * k).start()
+
+    each(0, chip, relay)
+
     top_buf[...] = jnp.full(top_buf.shape, -jnp.inf, F32)
     norm_buf[...] = jnp.zeros(norm_buf.shape, F32)
     outt_buf[...] = jnp.zeros(outt_buf.shape, F32)
 
     def forward(j):
-        for d in (2 * j, 2 * j + 1):
-
-            @pl.when(d != me)
-            def _():
-                kv_copy(d, sib).wait_recv()
-
+        kv_copy(2 * j + 1 - core, sib).wait_recv()
         at = pl.multiple_of(j * block, block)
         keys = kv_all[pl.ds(at, block), :HEAD_WIDTH]
         values_t = kv_all[pl.ds(at, block), HEAD_WIDTH:].T
@@ -383,12 +393,6 @@
             dkv_own[:, :HEAD_WIDTH] = jnp.where(own, key_acc[:rows], key_acc[rows:])
             dkv_own[:, HEAD_WIDTH:] = jnp.where(own, value_acc[:rows], value_acc[rows:])
 
-        for d in (2 * j, 2 * j + 1):
-
-            @pl.when(d < me)
-            def _():
-                dkv_copy(me, d).start()
-
     each(0, chip + 1, backward)
 
     s_acc[...] = jnp.zeros(s_acc.shape, F32)
@@ -401,41 +405,54 @@
 
     each(0, n, wait_tot)
 
-    def fold(acc, buf, rsem, src_ref, k):
-        chip_copy(src_ref, buf, rsem, rsem, k, chip).wait_recv()
+    def fold(acc, buf, rsem, src_ref, i, k):
+        chip_copy(src_ref, buf, rsem, rsem, k, chip, i).wait_recv()
         grow = jnp.exp(total_of(2 * k) + total_of(2 * k + 1))
-        for h in range(half_heads):
+        for h in range(i * heads_piece, (i + 1) * heads_piece):
             at = slice(h * width, (h + 1) * width)
             acc[at, :] = grow[h : h + 1, :] * acc[at, :] + buf[k, at, :].astype(F32)
 
-    each(0, chip, lambda k: fold(s_acc, fw_buf, fw_r, u_chip, k))
-    each(
-        0,
-        chips - 1 - chip,
-        lambda i: fold(a_acc, bw_buf, bw_r, t_chip, chips - 1 - i),
-    )
-    for h in range(half_heads):
-        at = slice(h * width, (h + 1) * width)
-        mine_at = pl.ds(pl.multiple_of(my_half + h * width, width), width)
-        even_u, _ = pair_of(u_own, u_sib, h)
-        state_even = s_acc[at, :]
-        state_odd = grow_even[h : h + 1, :] * state_even + even_u
-        s_full[mine_at, :] = jnp.where(first, state_even, state_odd).astype(BF16)
-        s_send[at, :] = jnp.where(first, state_odd, state_even).astype(BF16)
-        _, odd_t = pair_of(t_own, t_sib, h)
-        adj_odd = a_acc[at, :]
-        adj_even = grow_odd[h : h + 1, :] * adj_odd + odd_t
-        a_full[mine_at, :] = jnp.where(first, adj_even, adj_odd).astype(BF16)
-        a_send[at, :] = jnp.where(first, adj_odd, adj_even).astype(BF16)
-    back_s = sib_copy(s_send, s_full.at[pl.ds(my_half, half)], 2)
-    back_a = sib_copy(a_send, a_full.at[pl.ds(my_half, half)], 3)
-    back_s.start()
-    back_a.start()
-
-    sib_copy(s_send, s_full.at[pl.ds(sib_half, half)], 2).wait_recv()
-    sib_copy(a_send, a_full.at[pl.ds(sib_half, half)], 3).wait_recv()
-    rw_acc[:, n_state:] = rw_acc[:, n_state:] + dot(us_buf[...], s_full[...], 1, 0)
-    rw_acc[:, :n_state] = rw_acc[:, :n_state] + dot(xs_buf[...], a_full[...], 1, 0)
+    def back_pieces(i, base):
+        span = pl.ds(i * piece, piece)
+        return (
+            sib_copy(s_send.at[span], s_full.at[part_rows(base, i)], 4 * i + 2),
+            sib_copy(a_send.at[span], a_full.at[part_rows(base, i)], 4 * i + 3),
+        )
+
+    def add_states(i):
+        for copy in back_pieces(i, sib_half):
+            copy.wait_recv()
+        for at in (i * piece, half + i * piece):
+            span = slice(at, at + piece)
+            rw_acc[:, n_state:] = rw_acc[:, n_state:] + dot(us_buf[:, span], s_full[span, :], 1, 0)
+            rw_acc[:, :n_state] = rw_acc[:, :n_state] + dot(xs_buf[:, span], a_full[span, :], 1, 0)
+
+    for i in range(PIECES):
+        each(0, chip, lambda k: fold(s_acc, fw_buf, fw_r, u_chip, i, k))
+        each(
+            0,
+            chips - 1 - chip,
+            lambda k: fold(a_acc, bw_buf, bw_r, t_chip, i, chips - 1 - k),
+        )
+        for h in range(i * heads_piece, (i + 1) * heads_piece):
+            at = slice(h * width, (h + 1) * width)
+            mine_at = pl.ds(pl.multiple_of(my_half + h * width, width), width)
+            even_u, _ = pair_of(u_own, u_sib, h)
+            state_even = s_acc[at, :]
+            state_odd = grow_even[h : h + 1, :] * state_even + even_u
+            s_full[mine_at, :] = jnp.where(first, state_even, state_odd).astype(BF16)
+            s_send[at, :] = jnp.where(first, state_odd, state_even).astype(BF16)
+            _, odd_t = pair_of(t_own, t_sib, h)
+            adj_odd = a_acc[at, :]
+            adj_even = grow_odd[h : h + 1, :] * adj_odd + odd_t
+            a_full[mine_at, :] = jnp.where(first, adj_even, adj_odd).astype(BF16)
+            a_send[at, :] = jnp.where(first, adj_odd, adj_even).astype(BF16)
+        for copy in back_pieces(i, my_half):
+            copy.start()
+        if i > 0:
+            add_states(i - 1)
+    add_states(PIECES - 1)
+
     rs_send[...] = rw_acc[...].astype(BF16)
 
     def send_rs(d):
@@ -444,6 +461,7 @@
             rs_copy(grp, d).start()
 
     each(0, ng, send_rs)
+    each(0, me, lambda d: dkv_copy(me, d).start())
     so_ref[...] = (
         so_ref[...].astype(F32) + heads_buf[...] * dot(rd_ref[...], s_full[...], 1, 1)
     ).astype(BF16)
@@ -496,21 +514,23 @@
         def _():
             tot_copy(me, d).wait_send()
 
-            @pl.when(d >= 2 * chip)
-            def _():
-                kv_copy(me, d).wait_send()
-
             @pl.when(d < me)
             def _():
                 dkv_copy(me, d).wait_send()
 
     each(0, n, end_ctx)
-    sib_u.wait_send()
-    sib_t.wait_send()
-    back_s.wait_send()
-    back_a.wait_send()
-    each(chip + 1, chips, lambda d: chip_copy(u_chip, fw_buf, fw_s, fw_r, chip, d).wait_send())
-    each(0, chip, lambda d: chip_copy(t_chip, bw_buf, bw_s, bw_r, chip, d).wait_send())
+    kv_copy(me, sib).wait_send()
+    each(chip + 1, chips, lambda k: kv_copy(me, 2 * k + core).wait_send())
+    each(0, chip, lambda k: kv_copy(2 * k + core, sib, 2 * k).wait_send())
+    for i in range(PIECES):
+        for copy in sib_pieces(i) + back_pieces(i, my_half):
+            copy.wait_send()
+        each(
+            chip + 1,
+            chips,
+            lambda d: chip_copy(u_chip, fw_buf, fw_s, fw_r, chip, d, i).wait_send(),
+        )
+        each(0, chip, lambda d: chip_copy(t_chip, bw_buf, bw_s, bw_r, chip, d, i).wait_send())
 
     def end_grp(d):
         @pl.when(d != grp)
@@ -602,12 +622,12 @@
             dma((n,)),
             dma((n,)),
             dma((n,)),
-            dma((4,)),
-            dma((4,)),
-            dma((chips,)),
-            dma((chips,)),
-            dma((chips,)),
-            dma((chips,)),
+            dma((4 * PIECES,)),
+            dma((4 * PIECES,)),
+            dma((chips, PIECES)),
+            dma((chips, PIECES)),
+            dma((chips, PIECES)),
+            dma((chips, PIECES)),
             dma((n,)),
             dma((n,)),
             dma((ng,)),

time: 44.4 us -> 39.8 us (0.90)
  Pallas kernels: 43.6 us -> 38.7 us
    pallas_call x1, Pallas kernels: 41.3 us -> 36.5 us  [on_device(): pl.pallas_call(functools.partial(kernel, n, ng), out_shape=(jax.ShapeDtyp...]
where the time goes in v3:
time: 39.8 us; the launch traced here: 39.4 us
  Pallas kernels  38.7 us (97%)
  between operations  0.64 us (2%)
    pallas_call x1, Pallas kernels, on_device(): pl.pallas_call(functools.partial(kernel, n, ng), out_shape=(jax.ShapeDtyp...  36.5 us
    pallas_call x1, Pallas kernels, on_device(): pl.pallas_call(store, out_shape=(jax.ShapeDtypeStruct((rows, cols), BF16)...  2.27 us

profile of v3, /device:TPU:4, one launch (start us, length us, event | category | flops | bytes accessed | tf_op | source)
XLA Modules:
  0.0 39.4 jit_solution(16612253094522949771)
XLA Ops:
  0.6 36.5 %shard_map.135 = (bf16[128,1024]{1,0:T(8,128)(2,1)}, bf16[128,1024]{1,0:T(8,128)(2,1)}, bf16[128,256]{1,0:T(8,128)(2,1)}, bf16[128,1024]{1,0:T(8,128)(2,1)}, bf1...) custom-call(bf16[128,1024]{1,0:T(8,128)(2,1)} %q_ref.1, bf16[128,2,128]{2,1,0:T(2,128)(2,1)} %kv_ref.1, ...), custom_call_target="tpu_custom_call" | custom-call | tf_op jit(solution)/shard_map/pallas_call | solution.py:575
  37.1 2.3 %shard_map.136 = (bf16[128,1024]{1,0:T(8,128)(2,1)}, bf16[128,1024]{1,0:T(8,128)(2,1)}, bf16[128,2,128]{2,1,0:T(2,128)(2,1)}, bf16[128,1024]{1,0:T(8,128)(2,1)},...) custom-call(bf16[128,1024]{1,0:T(8,128)(2,1)} %get-tuple-element.14.refs_0_, ...), custom_call_target="tpu_custom_call" | custom-call | tf_op jit(solution)/shard_map/pallas_call | solution.py:651
